TPU v7x, 32 devices: a whole 2x2x4 slice. The times are simulated.
32 devices in a mesh: groups: 2 (over y), ctx: 4 (over z), tp: 4 (over x, core).
Axes of the slice: x: 2, y: 2, z: 4, core: 2. Of those that a mesh axis runs over, the one named last changes fastest.
Arguments:
- queries: bfloat16 [1024, 8192], P(('groups', 'ctx'), 'tp'), parts along dimension 0, may hold values from -5 to 5
- suffix_keys_values: bfloat16 [2, 1024, 1024], P(None, ('groups', 'ctx'), 'tp'), parts along dimension 1, may hold values from -5 to 5
- cached_page_pool: bfloat16 [2, 256, 16, 1024], P(None, ('groups', 'ctx'), None, 'tp'), parts along dimension 1, may hold values from -5 to 5
- prefix_page_hits: int32 [8, 32], P('groups'), parts along dimension 0, may hold values from 0 to 127, as said below
- lengths: int32 [8], P('groups'), parts along dimension 0, may hold values from 1 to 256, 512 in all
- mamba_x: bfloat16 [1024, 8192], P(('groups', 'ctx'), 'tp'), parts along dimension 0, may hold values from -5 to 5
- gate_z: bfloat16 [1024, 8192], P(('groups', 'ctx'), 'tp'), parts along dimension 0, may hold values from -6 to 6
- delta: bfloat16 [1024, 8192], P(('groups', 'ctx'), 'tp'), parts along dimension 0, may hold values from -7 to 1.024
- b_c: float32 [2, 16, 1024], P(None, None, ('groups', 'ctx')), parts along dimension 2, may hold values from -5 to 5
- a_log: float32 [16, 8192], P(None, 'tp'), may hold values from -6 to 4
- d_skip: float32 [8192], P('tp'), may hold values from 0.5 to 1.5
- state_pool: float32 [16, 16, 8192], P(('groups', 'ctx'), None, 'tp'), parts along dimension 0, may hold values from -3 to 3
- state_hits: int32 [8], P('groups'), parts along dimension 0, may hold values from 0 to 7, as said below
Outputs:
- attention_out: bfloat16 [1024, 8192], P(('groups', 'ctx'), 'tp'), parts along dimension 0
- mamba_out: bfloat16 [1024, 8192], P(('groups', 'ctx'), 'tp'), parts along dimension 0
There are 2 independent parts, one for each index of `groups`. A program takes and returns all parts, laid end to end along the dimension named above; an argument that names none is the same for every part. Nothing has to cross between parts.
Inputs may be any that keep to these rules, and one draw needn't show every extreme that they name: `prefix_page_hits`: page p is held by ctx device p // 32; a request's 32 pages are distinct, requests may share pages. `state_hits`: slot s is held by ctx device s // 2; requests have distinct slots.
All inputs are finite; a program needn't handle non-finite values.
Results may differ from a plain program's by a relative error of at most 0.007.
Values may be sent and summed in bfloat16 or wider, within the bound.
A program may use at most 128 MiB of HBM per device.

v0:
```python
import math

import jax
import jax.numpy as jnp
from jax import lax
from jax.sharding import PartitionSpec as P

PER_HEAD_DIM = 128


FLOOR_SCORE = -1e30


def entering(shard, axis, join, neutral):
    place = lax.axis_index(axis)
    gathered = jax.tree.map(
        lambda a, kind: lax.all_gather(a.astype(kind), axis),
        shard,
        jax.tree.map(lambda a: jnp.bfloat16 if a.dtype == jnp.float32 else a.dtype, shard),
    )
    state = jax.tree.map(lambda a, e: jnp.zeros_like(a) + jnp.asarray(e, a.dtype), shard, neutral)

    def one(turn, state):
        return join(
            state,
            jax.tree.map(
                lambda a, own: lax.dynamic_index_in_dim(a, turn, 0, False).astype(own.dtype),
                gathered,
                shard,
            ),
        )

    return lax.fori_loop(0, place, one, state)


def segments_of(positions, lengths):
    ends = jnp.cumsum(lengths)
    starts = ends - lengths
    member = (positions[:, None] >= starts[None, :]).astype(jnp.int32)
    return (jnp.sum(member, axis=1) - 1, starts)


def attend_block(status, grouped, key_block, value_block, visible, scale):
    largest, weight_sum, accum = status
    scores = (
        jnp.einsum("tgqd,kgd->tgqk", grouped, key_block, preferred_element_type=jnp.float32) * scale
    )
    shown = visible[:, None, None, :]
    scores = jnp.where(shown, scores, FLOOR_SCORE)
    new_largest = jnp.maximum(largest, jnp.max(scores, axis=-1))
    weights = jnp.where(shown, jnp.exp(scores - new_largest[..., None]), 0.0)
    multiplier = jnp.exp(largest - new_largest)
    weight_sum = weight_sum * multiplier + jnp.sum(weights, axis=-1)
    update = jnp.einsum(
        "tgqk,kgd->tgqd",
        weights.astype(jnp.bfloat16),
        value_block,
        preferred_element_type=jnp.float32,
    )
    return (new_largest, weight_sum, accum * multiplier[..., None] + update)


def fold_keys(status, grouped, address_line_indices, value_row_list, visible_fn, shard_keys, scale):
    key_count = address_line_indices.shape[0]
    block_size = math.gcd(key_count, max(shard_keys, 512))
    block_count = key_count // block_size

    def fold_advance(current, block_idx):
        offset = block_idx * block_size
        key_block = lax.dynamic_slice_in_dim(address_line_indices, offset, block_size, 0)
        value_block = lax.dynamic_slice_in_dim(value_row_list, offset, block_size, 0)
        visible = visible_fn(offset, block_size)
        current = attend_block(current, grouped, key_block, value_block, visible, scale)
        return (current, None)

    status, _ = lax.scan(fold_advance, status, jnp.arange(block_count, dtype=jnp.int32))
    return status


def attention_layer(
    queries, suffix_keys_values, cached_page_pool, prefix_page_hits, lengths, positions, segment
):
    token_count = queries.shape[0]
    kv_width = suffix_keys_values.shape[2]
    groups_local = kv_width // PER_HEAD_DIM
    group_share = queries.shape[1] // kv_width
    scale = 1.0 / math.sqrt(PER_HEAD_DIM)
    grouped = queries.reshape(token_count, groups_local, group_share, PER_HEAD_DIM)
    status = (
        jnp.full((token_count, groups_local, group_share), FLOOR_SCORE, jnp.float32),
        jnp.zeros((token_count, groups_local, group_share), jnp.float32),
        jnp.zeros((token_count, groups_local, group_share, PER_HEAD_DIM), jnp.float32),
    )
    page_len = cached_page_pool.shape[2]
    pool_local = cached_page_pool.shape[1]
    request_hits = jnp.take(prefix_page_hits, segment, axis=0)

    def add_pages(current, piece):
        cache_keys = piece[0].reshape(-1, groups_local, PER_HEAD_DIM)
        cache_values = piece[1].reshape(-1, groups_local, PER_HEAD_DIM)

        def pool_visible(first_key, block_size):
            page_ids = (first_key + jnp.arange(block_size, dtype=jnp.int32)) // page_len
            return jnp.any(request_hits[:, :, None] == page_ids[None, None, :], axis=1)

        return fold_keys(
            current, grouped, cache_keys, cache_values, pool_visible, pool_local * page_len, scale
        )

    status = add_pages(status, lax.all_gather(cached_page_pool, "ctx", axis=1, tiled=True))

    def add_suffix(current, piece):
        suffix_keys = piece[0].reshape(-1, groups_local, PER_HEAD_DIM)
        suffix_values = piece[1].reshape(-1, groups_local, PER_HEAD_DIM)

        def suffix_visible(first_key, block_size):
            key_pos = first_key + jnp.arange(block_size, dtype=jnp.int32)
            key_segment, _ = segments_of(key_pos, lengths)
            return (segment[:, None] == key_segment[None, :]) & (
                key_pos[None, :] <= positions[:, None]
            )

        return fold_keys(
            current, grouped, suffix_keys, suffix_values, suffix_visible, token_count, scale
        )

    status = add_suffix(status, lax.all_gather(suffix_keys_values, "ctx", axis=1, tiled=True))
    largest, weight_sum, accum = status
    return (accum / weight_sum[..., None]).reshape(token_count, -1).astype(jnp.bfloat16)


def chain_combine(earlier, later):
    return (earlier[0] * later[0], later[0] * earlier[1] + later[1])


def mamba_layer(
    mamba_x, gate_z, delta, b_c, a_log, d_skip, state_pool, state_hits, positions, segment, starts
):
    token_count = mamba_x.shape[0]
    slot_count = state_pool.shape[0]
    local_slots = state_hits - lax.axis_index("ctx") * slot_count
    is_held = (local_slots >= 0) & (local_slots < slot_count)
    chosen = jnp.take(state_pool, jnp.clip(local_slots, 0, slot_count - 1), axis=0)
    initial = lax.psum(
        jnp.where(is_held[:, None, None], chosen, 0.0).astype(jnp.bfloat16), "ctx"
    ).astype(jnp.float32)
    rate = -jnp.exp(a_log)
    step_size = jax.nn.softplus(delta.astype(jnp.float32))
    inputs = mamba_x.astype(jnp.float32)
    opening = jnp.any(positions[:, None] == starts[None, :], axis=1)
    request_count = starts.shape[0]
    selector = (
        (segment[:, None] == jnp.arange(request_count, dtype=jnp.int32)[None, :]) & opening[:, None]
    ).astype(jnp.float32)
    block_size = math.gcd(token_count, 8)
    block_count = token_count // block_size
    in_proj = b_c[0].T
    out_proj = b_c[1].T
    rows_idx = jnp.arange(block_size, dtype=jnp.int32)
    lower = (rows_idx[None, :] <= rows_idx[:, None]).astype(jnp.float32)

    def blocked(array):
        return array.reshape((block_count, block_size) + array.shape[1:])

    def mamba_advance(carry, pieces):
        step_blk, input_blk, in_blk, out_blk, select_blk, open_blk = pieces
        log_decay = step_blk[:, None, :] * rate[None, :, :]
        decay = jnp.exp(log_decay)
        drive = step_blk[:, None, :] * in_blk[:, :, None] * input_blk[:, None, :]
        begun = jnp.einsum("tr,rnd->tnd", select_blk, initial, precision=lax.Precision.HIGHEST)
        drive = drive + decay * begun
        running = jnp.einsum("ts,snd->tnd", lower, log_decay, precision=lax.Precision.HIGHEST)
        opened = jnp.einsum(
            "ts,s->t", lower, open_blk.astype(jnp.float32), precision=lax.Precision.HIGHEST
        )
        linked = (opened[:, None] == opened[None, :]) & (lower > 0.5)
        gap = jnp.where(linked[:, :, None, None], running[:, None] - running[None, :], -jnp.inf)
        within = jnp.sum(jnp.exp(gap) * drive[None], axis=1)
        carry_decay, carry_drive, carry_mark = carry
        leading_blk = (opened < 0.5)[:, None, None]
        from_start = jnp.exp(running)
        joined_decay = jnp.where(leading_blk, carry_decay[None] * from_start, 0.0)
        joined_drive = within + jnp.where(leading_blk, from_start * carry_drive[None], 0.0)
        partial_out = jnp.einsum(
            "tn,tnd->td", out_blk, joined_drive, precision=lax.Precision.HIGHEST
        )
        new_carry = (
            joined_decay[-1],
            joined_drive[-1],
            jnp.maximum(carry_mark, jnp.minimum(opened[-1], 1.0)),
        )
        return (new_carry, (joined_decay, partial_out))

    start_carry = (
        jnp.ones(rate.shape, jnp.float32),
        jnp.zeros(rate.shape, jnp.float32),
        jnp.zeros((), jnp.float32),
    )
    final, (decays_all, partial_all) = lax.scan(
        mamba_advance,
        start_carry,
        (
            blocked(step_size),
            blocked(inputs),
            blocked(in_proj),
            blocked(out_proj),
            blocked(selector),
            blocked(opening),
        ),
    )
    last_decay, last_drive, any_open = final
    outgoing = (jnp.where(any_open > 0.5, 0.0, last_decay), last_drive)
    incoming = entering(
        outgoing, "ctx", chain_combine, (jnp.ones_like(last_decay), jnp.zeros_like(last_drive))
    )[1]
    decays_all = decays_all.reshape((token_count,) + rate.shape)
    leading = jnp.cumsum(opening.astype(jnp.int32)) == 0
    carried = jnp.einsum(
        "tn,tnd,nd->td", out_proj, decays_all, incoming, precision=lax.Precision.HIGHEST
    )
    reply = (
        partial_all.reshape(token_count, -1)
        + jnp.where(leading[:, None], carried, 0.0)
        + d_skip[None, :] * inputs
    )
    return (reply * jax.nn.silu(gate_z.astype(jnp.float32))).astype(jnp.bfloat16)


def local(
    queries,
    suffix_keys_values,
    cached_page_pool,
    prefix_page_hits,
    lengths,
    mamba_x,
    gate_z,
    delta,
    b_c,
    a_log,
    d_skip,
    state_pool,
    state_hits,
):
    token_count = queries.shape[0]
    positions = lax.axis_index("ctx") * token_count + jnp.arange(token_count, dtype=jnp.int32)
    segment, starts = segments_of(positions, lengths)
    attended = attention_layer(
        queries, suffix_keys_values, cached_page_pool, prefix_page_hits, lengths, positions, segment
    )
    mixed = mamba_layer(
        mamba_x,
        gate_z,
        delta,
        b_c,
        a_log,
        d_skip,
        state_pool,
        state_hits,
        positions,
        segment,
        starts,
    )
    return (attended, mixed)


def solution(mesh):
    placed = (
        P(("groups", "ctx"), "tp"),
        P(None, ("groups", "ctx"), "tp"),
        P(None, ("groups", "ctx"), None, "tp"),
        P("groups", None),
        P("groups"),
        P(("groups", "ctx"), "tp"),
        P(("groups", "ctx"), "tp"),
        P(("groups", "ctx"), "tp"),
        P(None, None, ("groups", "ctx")),
        P(None, "tp"),
        P("tp"),
        P(("groups", "ctx"), None, "tp"),
        P("groups"),
    )
    return jax.shard_map(
        local,
        mesh=mesh,
        in_specs=placed,
        out_specs=(P(("groups", "ctx"), "tp"), P(("groups", "ctx"), "tp")),
        check_vma=False,
    )
```

profile of v0, /device:TPU:30, one launch (start us, length us, event | category | flops | bytes accessed | tf_op | source)
XLA Modules:
  0.0 377.9 jit_solution(9544172893939609056)
XLA Ops:
  14.4 2.6 fusion.59
  18.8 15.5 %all_gather.19 = bf16[2,512,256]{1,2,0:T(8,128)(2,1)S(1)} all-gather(bf16[2,128,256]{1,2,0:T(8,128)(2,1)S(1)} %copy.66), channel_id=1, replica_groups=mesh['groups'=2,'ctx'=4,'tp'=4] {'ctx'}, dimensions={1}, use_global_device_ids=true | all-gather | bytes 655360 | tf_op jit(solution)/shard_map/all_gather | solution.py:127
  35.8 2.7 fusion.37
  38.5 9.8 %all-reduce.2.cloned.1.call-done = bf16[4,16,2048]{2,1,0:T(8,128)(2,1)} async-done(((bf16[4,16,2048]{2,1,0:T(8,128)(2,1)}), bf16[4,16,2048]{2,1,0:T(8,128)(2,1)}) %all-reduce.2.cloned.1.call-update) | async-done | bytes 262160 | tf_op jit(solution)/shard_map/psum | solution.py:144
  49.5 208.6 %while.56 = (s32[]{:T(128)}, f32[16,2048]{1,0:T(8,128)S(1)}, f32[16,2048]{1,0:T(8,128)S(1)}, f32[]{:T(128)}, f32[16,8,16,2048]{3,2,1,0:T(8,128)}, /*index=5*/f32...) while((s32[]{:T(128)}, f32[16,2048]{1,0:T(8,128)S(1)}, ...), condition=%wide.region_14.15_spmd.clone.clone, body=%wide.region_12.14_spmd.clone.clone.sunk | while | flops 51905864 | bytes 19545496 | solution.py:199
  54.4 2.2 multiply_reduce_fusion.2
  57.5 1.6 copy_dynamic-update-slice_fusion.2
  67.4 2.2 multiply_reduce_fusion.2
  70.5 1.7 copy_dynamic-update-slice_fusion.2
  80.5 2.2 multiply_reduce_fusion.2
  93.5 2.2 multiply_reduce_fusion.2
  106.5 2.2 multiply_reduce_fusion.2
  119.5 2.2 multiply_reduce_fusion.2
  122.7 1.6 copy_dynamic-update-slice_fusion.2
  132.6 2.2 multiply_reduce_fusion.2
  135.7 1.6 copy_dynamic-update-slice_fusion.2
  145.6 2.2 multiply_reduce_fusion.2
  158.7 2.2 multiply_reduce_fusion.2
  161.8 1.7 copy_dynamic-update-slice_fusion.2
  171.8 2.2 multiply_reduce_fusion.2
  184.8 2.2 multiply_reduce_fusion.2
  197.8 2.2 multiply_reduce_fusion.2
  210.8 2.2 multiply_reduce_fusion.2
  213.9 1.7 copy_dynamic-update-slice_fusion.2
  223.9 2.2 multiply_reduce_fusion.2
  236.9 2.2 multiply_reduce_fusion.2
  249.9 2.2 multiply_reduce_fusion.2
  253.1 1.6 copy_dynamic-update-slice_fusion.2
  258.1 14.7 %all-gather = bf16[64,2048]{1,0:T(8,128)(2,1)S(1)} all-gather(bf16[16,2048]{1,0:T(8,128)(2,1)S(1)} %select_convert_fusion.1), channel_id=2, replica_groups=mesh['groups'=2,'ctx'=4,'tp'=4] {'ctx'}, dimensions={0}, use_global_device_ids=true | all-gather | bytes 327680 | tf_op jit(solution)/shard_map/all_gather | solution.py:17
  272.9 14.5 %all-gather.1 = bf16[64,2048]{1,0:T(8,128)(2,1)S(1)} all-gather(bf16[16,2048]{1,0:T(8,128)(2,1)S(1)} %convert_element_type.100), channel_id=3, replica_groups=mesh['groups'=2,'ctx'=4,'tp'=4] {'ctx'}, dimensions={0}, use_global_device_ids=true | all-gather | bytes 327680 | tf_op jit(solution)/shard_map/all_gather | solution.py:17
  287.6 6.8 %bitcast_multiply_fusion = f32[128,16,2048]{2,1,0:T(8,128)S(1)} fusion(f32[16,8,16,2048]{3,2,1,0:T(8,128)} %get-tuple-element.283, f32[16,2048]{1,0:T(8,128)S(1)} %get-tuple-element.287), kind=kLoop, calls=%fused_computation.70 | loop fusion | flops 4194304 | bytes 33685504 | tf_op jit(solution)/shard_map/tn,tnd,nd->td/dot_general | solution.py:218
  294.5 9.5 %fusion.35 = f32[128,1,2048]{2,1,0:T(1,128)S(1)} fusion(f32[128,16,1]{1,2,0:T(1,128)S(1)} %copy.86, f32[128,16,2048]{2,1,0:T(8,128)S(1)} %bitcast_multiply_fusion), kind=kOutput, calls=%fused_computation.68 | convolution fusion | flops 50331648 | bytes 17833984 | tf_op jit(solution)/shard_map/tn,tnd,nd->td/dot_general | solution.py:218
  305.6 2.7 fusion.71
  309.9 54.2 %while.57 = (s32[]{:T(128)}, f32[128,2,8]{0,2,1:T(8,128)S(1)}, f32[128,2,8]{0,2,1:T(8,128)S(1)}, f32[128,2,8,128]{0,3,2,1:T(8,128)}, s32[128,32]{1,0:T(8,128)S(1...) while((s32[]{:T(128)}, f32[128,2,8]{0,2,1:T(8,128)S(1)}, ...), condition=%wide.region_6.7_spmd.clone, body=%wide.region_2.0_spmd.clone.sunk | while | flops 555436032 | bytes 17846476 | solution.py:76
  312.8 2.7 fusion.106
  315.5 3.2 fusion.107
  318.8 4.4 %fusion.109 = f32[128,2,8,128]{0,3,2,1:T(8,128)} fusion(f32[2,512,128,8]{2,1,3,0:T(8,128)} %get-tuple-element.712, f32[128,2,8]{0,2,1:T(8,128)S(1)} %select_maximum_fusion.2, pred[128,512]{0,1:T(8,128)(4,1)S(1)} %copy.134, f32[128,2,8,128]{0,3,2,1:T(8,128)} %get-tuple-element.732, f32[128,2,8]{0,2,1:T(8,128)S(1)} %get-tuple-element.714, ...), kind=kOutput, calls=%fused_computation.45.clone.1 | convolution fusion | flops 274464768 | bytes 6635521 | tf_op jit(solution)/shard_map/while/body/eval_jaxpr/tgqk,kgd->tgqd/dot_general | solution.py:54
  326.1 2.7 fusion.106
  328.8 3.2 fusion.107
  332.2 4.7 %fusion.109 = f32[128,2,8,128]{0,3,2,1:T(8,128)} fusion(f32[2,512,128,8]{2,1,3,0:T(8,128)} %get-tuple-element.712, f32[128,2,8]{0,2,1:T(8,128)S(1)} %select_maximum_fusion.2, pred[128,512]{0,1:T(8,128)(4,1)S(1)} %copy.134, f32[128,2,8,128]{0,3,2,1:T(8,128)} %get-tuple-element.732, f32[128,2,8]{0,2,1:T(8,128)S(1)} %get-tuple-element.714, ...), kind=kOutput, calls=%fused_computation.45.clone.1 | convolution fusion | flops 274464768 | bytes 6635521 | tf_op jit(solution)/shard_map/while/body/eval_jaxpr/tgqk,kgd->tgqd/dot_general | solution.py:54
  339.7 2.7 fusion.106
  342.4 3.2 fusion.107
  345.8 4.7 %fusion.109 = f32[128,2,8,128]{0,3,2,1:T(8,128)} fusion(f32[2,512,128,8]{2,1,3,0:T(8,128)} %get-tuple-element.712, f32[128,2,8]{0,2,1:T(8,128)S(1)} %select_maximum_fusion.2, pred[128,512]{0,1:T(8,128)(4,1)S(1)} %copy.134, f32[128,2,8,128]{0,3,2,1:T(8,128)} %get-tuple-element.732, f32[128,2,8]{0,2,1:T(8,128)S(1)} %get-tuple-element.714, ...), kind=kOutput, calls=%fused_computation.45.clone.1 | convolution fusion | flops 274464768 | bytes 6635521 | tf_op jit(solution)/shard_map/while/body/eval_jaxpr/tgqk,kgd->tgqd/dot_general | solution.py:54
  353.4 2.7 fusion.106
  356.0 3.2 fusion.107
  359.4 4.7 %fusion.109 = f32[128,2,8,128]{0,3,2,1:T(8,128)} fusion(f32[2,512,128,8]{2,1,3,0:T(8,128)} %get-tuple-element.712, f32[128,2,8]{0,2,1:T(8,128)S(1)} %select_maximum_fusion.2, pred[128,512]{0,1:T(8,128)(4,1)S(1)} %copy.134, f32[128,2,8,128]{0,3,2,1:T(8,128)} %get-tuple-element.732, f32[128,2,8]{0,2,1:T(8,128)S(1)} %get-tuple-element.714, ...), kind=kOutput, calls=%fused_computation.45.clone.1 | convolution fusion | flops 274464768 | bytes 6635521 | tf_op jit(solution)/shard_map/while/body/eval_jaxpr/tgqk,kgd->tgqd/dot_general | solution.py:54
  364.1 3.3 fusion.38
  367.5 2.6 divide_convert_fusion
  (419 shorter events, 175.0 us)
Async XLA Ops:
  7.2 1.0 copy-start
  7.2 9.8 %copy-start.8 = (f32[16,2048]{1,0:T(8,128)S(1)}, f32[16,2048]{1,0:T(8,128)}, u32[]{:S(2)}) copy-start(f32[16,2048]{1,0:T(8,128)} %param.28) | copy-start | bytes 393220
  7.2 10.7 %copy-start.6 = (bf16[128,2048]{1,0:T(8,128)(2,1)S(1)}, bf16[128,2048]{1,0:T(8,128)(2,1)}, u32[]{:S(2)}) copy-start(bf16[128,2048]{1,0:T(8,128)(2,1)} %param.19) | copy-start | bytes 1572868
  7.2 11.4 %copy-start.9 = (bf16[2,128,256]{2,1,0:T(8,128)(2,1)S(1)}, bf16[2,128,256]{2,1,0:T(8,128)(2,1)}, u32[]{:S(2)}) copy-start(bf16[2,128,256]{2,1,0:T(8,128)(2,1)} %param.20) | copy-start | bytes 393220
  7.2 41.1 %all-reduce.2.cloned.1.call-start = ((), (), s32[]{:S(2)}) async-start(), calls=%async_computation.1 | async-start | bytes 524288 | tf_op jit(solution)/shard_map/psum | solution.py:144
  9.6 296.0 %all-gather.4.cloned.1.call-start = ((), (), s32[]{:S(2)}) async-start(), calls=%async_computation | async-start | bytes 2621440 | tf_op jit(solution)/shard_map/all_gather | solution.py:110
  12.3 22.7 %copy-start.2 = (s32[4,32]{1,0:T(4,128)S(1)}, s32[4,32]{1,0:T(4,128)}, u32[]{:S(2)}) copy-start(s32[4,32]{1,0:T(4,128)} %param.22) | copy-start | bytes 1540
  294.5 9.6 %copy-start.4 = (bf16[128,2048]{1,0:T(8,128)(2,1)S(1)}, bf16[128,2048]{1,0:T(8,128)(2,1)}, u32[]{:S(2)}) copy-start(bf16[128,2048]{1,0:T(8,128)(2,1)} %param.24) | copy-start | bytes 1572868
  294.5 9.6 %copy-start.5 = (f32[16,8,2048]{2,1,0:T(8,128)S(1)}, f32[16,8,2048]{2,1,0:T(8,128)}, u32[]{:S(2)}) copy-start(f32[16,8,2048]{2,1,0:T(8,128)} %get-tuple-element.282) | copy-start | bytes 3145732
  294.5 9.6 %copy-start.7 = (bf16[128,2048]{1,0:T(8,128)(2,1)S(1)}, bf16[128,2048]{1,0:T(8,128)(2,1)}, u32[]{:S(2)}) copy-start(bf16[128,2048]{1,0:T(8,128)(2,1)} %param.25) | copy-start | bytes 1572868
  294.5 9.6 %copy-start.10 = (f32[2048]{0:T(1024)S(1)}, f32[2048]{0:T(1024)}, u32[]{:S(2)}) copy-start(f32[2048]{0:T(1024)} %param.29) | copy-start | bytes 24580
  364.1 3.4 copy-start.3
  367.4 3.7 copy-start.1
Sparse Core Ops, SparseCore 0:
  10.9 37.3 all-reduce.1
  49.9 44.6 all-gather.3
where the time goes:
time: 382 us; the launch traced here: 378 us
  matrix products  104 us (27%)
  local copies, waits for them, and re-layouts  101 us (26%)
  other arithmetic  87.8 us (23%)
  blocking collectives  44.7 us (12%)
  loops' own time  14.9 us (4%)
  between operations  14.4 us (4%)
  waiting for transfers between devices  10.5 us (3%)
    dynamic_update_slice x32, local copies, waits for them, and re-layouts, mamba_layer(): lax.scan(mamba_advance, start_carry, (blocked(step_size), blocked(inputs)...  36.1 us
    reduce_sum x16, other arithmetic, mamba_advance(): within = jnp.sum(jnp.exp(gap) * drive[None], axis=1)  35.8 us
    all_gather x2, blocking collectives, entering(): lax.all_gather(a.astype(kind), axis)  29.2 us
    dot_general x16, matrix products, mamba_advance(): jnp.einsum('tr,rnd->tnd', select_blk, initial, precision=lax.Precision.HI...  22.2 us
    dot_general x5, matrix products, attend_block(): jnp.einsum('tgqk,kgd->tgqd', weights.astype(jnp.bfloat16), value_block, p...  21 us
    dot_general x16, matrix products, mamba_advance(): jnp.einsum('tn,tnd->td', out_blk, joined_drive, precision=lax.Precision.H...  18.8 us
    dot_general x16, matrix products, mamba_advance(): jnp.einsum('ts,snd->tnd', lower, log_decay, precision=lax.Precision.HIGHEST)  17.2 us
    reduce_sum x5, other arithmetic, attend_block(): weight_sum = weight_sum * multiplier + jnp.sum(weights, axis=-1)  16 us
  transfers between devices with their start and end apart: 2, of which 1 were waited for; matrix products, arithmetic and copies ran while one was open for 60% of the time, Pallas kernels for 0%

commit v1 on v0

v1 whole, which is shorter than its diff:
```python
import functools
import math

import jax
import jax.numpy as jnp
from jax import lax
from jax.experimental import pallas as pl
from jax.experimental.pallas import tpu as pltpu
from jax.sharding import PartitionSpec as P

D = 128
LANES = 128
LOG2E = math.log2(math.e)
FLOOR = -1e30
VMEM = pl.BlockSpec(memory_space=pltpu.VMEM)
SMEM = pl.BlockSpec(memory_space=pltpu.SMEM)


def segments_of(positions, lengths):
    ends = jnp.cumsum(lengths)
    starts = ends - lengths
    member = (positions[:, None] >= starts[None, :]).astype(jnp.int32)
    return (jnp.sum(member, axis=1) - 1, starts)


def softplus(v):
    return jnp.maximum(v, 0.0) + jnp.log1p(jnp.exp(-jnp.abs(v)))


def spread_inputs(delta, x, a_log, dt_s, du_s, rate_s):
    tokens, width = delta.shape
    rows = width // LANES
    states = a_log.shape[0]
    for c in range(rows):
        cols = slice(c * LANES, (c + 1) * LANES)
        dt = softplus(delta[:, cols].astype(jnp.float32))
        dt_s[pl.ds(c, tokens, stride=rows), :] = dt
        du_s[pl.ds(c, tokens, stride=rows), :] = dt * x[:, cols].astype(jnp.float32)
        rate_s[pl.ds(c, states, stride=rows), :] = jnp.exp(a_log[:, cols]) * (-LOG2E)


def scan_tokens(tokens, rows, states, dt_s, du_s, rate_s, init_s, b_c, seg, opening, hs, y_s):
    def step(t, carry):
        hs, total = carry
        at = pl.ds(pl.multiple_of(t * rows, 8), rows)
        dt = dt_s[at, :]
        du = du_s[at, :]
        opens = opening[0, t] > 0
        r = seg[0, t]
        new, ys = [], []
        for n in range(states):
            part = slice(n * rows, (n + 1) * rows)
            prior = jnp.where(opens, init_s[r, part, :], hs[n])
            h = jnp.exp2(dt * rate_s[part, :]) * prior + du * b_c[n, t]
            new.append(h)
            if y_s is not None:
                ys.append(h * b_c[states + n, t])
        if y_s is not None:
            while len(ys) > 1:
                ys = [a + b for a, b in zip(ys[::2], ys[1::2])]
            y_s[at, :] = ys[0]
        return (tuple(new), total + dt)

    start = (tuple(hs), jnp.zeros((rows, LANES), jnp.float32))
    return lax.fori_loop(0, tokens, step, start, unroll=2)


def gate_outputs(x, gate, d_skip, y_s, out):
    tokens, width = x.shape
    rows = width // LANES
    for c in range(rows):
        cols = slice(c * LANES, (c + 1) * LANES)
        y = y_s[pl.ds(c, tokens, stride=rows), :]
        v = gate[:, cols].astype(jnp.float32)
        reply = y + d_skip[:, cols] * x[:, cols].astype(jnp.float32)
        out[:, cols] = (reply * (v / (1.0 + jnp.exp(-v)))).astype(out.dtype)


def load_initials(pool, hits, init_s, rows):
    count, states = init_s.shape[0], pool.shape[1]
    for r in range(count):
        chosen = pool[hits[0, r]].astype(jnp.float32)
        for c in range(rows):
            init_s[r, pl.ds(c, states, stride=rows), :] = chosen[:, c * LANES : (c + 1) * LANES]


def last_state_kernel(
    delta, x, a_log, pool, b_c, seg, opening, hits, last, dt_sum, dt_s, du_s, rate_s, init_s
):
    tokens, width = delta.shape
    rows, states = width // LANES, a_log.shape[0]
    spread_inputs(delta, x, a_log, dt_s, du_s, rate_s)
    load_initials(pool, hits, init_s, rows)
    zeros = [jnp.zeros((rows, LANES), jnp.float32)] * states
    hs, total = scan_tokens(
        tokens, rows, states, dt_s, du_s, rate_s, init_s, b_c, seg, opening, zeros, None
    )
    for n in range(states):
        last[n * rows : (n + 1) * rows, :] = hs[n]
    dt_sum[...] = total


def mamba_kernel(
    delta, x, a_log, gate, d_skip, pool, lasts, sums, b_c, seg, opening, hits, opened, place,
    out, dt_s, du_s, rate_s, init_s, y_s, enter_s,
):
    tokens, width = delta.shape
    rows, states = width // LANES, a_log.shape[0]
    spread_inputs(delta, x, a_log, dt_s, du_s, rate_s)
    load_initials(pool, hits, init_s, rows)
    enter_s[...] = jnp.zeros_like(enter_s)

    def join(j, carry):
        kept = jnp.where(opened[0, j] > 0, 0.0, 1.0)
        total = sums[j]
        for n in range(states):
            part = slice(n * rows, (n + 1) * rows)
            decay = jnp.exp2(total * rate_s[part, :]) * kept
            enter_s[part, :] = decay * enter_s[part, :] + lasts[j, part, :].astype(jnp.float32)
        return carry

    lax.fori_loop(0, place[0, 0], join, 0)
    hs = [enter_s[n * rows : (n + 1) * rows, :] for n in range(states)]
    scan_tokens(tokens, rows, states, dt_s, du_s, rate_s, init_s, b_c, seg, opening, hs, y_s)
    gate_outputs(x, gate, d_skip, y_s, out)


def attention_kernel(tile, block, q, suffix, pages, hits, starts, place, out, kept):
    tokens, width = q.shape
    kv_width = suffix.shape[3]
    heads_kv = kv_width // D
    share = width // kv_width
    requests, hit_count = hits.shape
    page_len = pages.shape[3]
    local_pages = pages.shape[2]
    per_shard = suffix.shape[2]
    first = place[0, 0] * tokens
    factor = LOG2E / math.sqrt(D)
    contract_last = (((1,), (1,)), ((), ()))
    rows = share * tile

    for r in range(requests):
        start, end = starts[0, r], starts[0, r + 1]

        @pl.when((start < first + tokens) & (end > first))
        def _():
            for j in range(hit_count):
                page = hits[r, j]
                shard, row = page // local_pages, page % local_pages
                for kind in range(2):
                    kept[kind, j * page_len : (j + 1) * page_len, :] = pages[shard, kind, row]
            for i in range(tokens // tile):
                low = first + i * tile

                @pl.when((start < low + tile) & (end > low))
                def _():
                    token = low + lax.rem(
                        lax.broadcasted_iota(jnp.int32, (rows, 1), 0), jnp.int32(tile)
                    )
                    mine = (token >= start) & (token < end)
                    for g in range(heads_kv):
                        cols = slice(g * D, (g + 1) * D)
                        span = slice(i * tile, (i + 1) * tile)
                        qt = jnp.concatenate(
                            [
                                q[span, (g * share + h) * D : (g * share + h + 1) * D]
                                for h in range(share)
                            ],
                            axis=0,
                        )
                        s = lax.dot_general(
                            qt, kept[0, :, cols], contract_last, preferred_element_type=jnp.float32
                        ) * factor
                        top = jnp.max(s, axis=1, keepdims=True)
                        w = jnp.exp2(s - top)
                        total = jnp.sum(w, axis=1, keepdims=True)
                        acc = jnp.dot(
                            w.astype(jnp.bfloat16),
                            kept[1, :, cols],
                            preferred_element_type=jnp.float32,
                        )

                        def fold(kb, carry):
                            top, total, acc = carry
                            shard = kb // (per_shard // block)
                            off = pl.multiple_of((kb % (per_shard // block)) * block, block)
                            k = suffix[shard, 0, pl.ds(off, block), cols]
                            v = suffix[shard, 1, pl.ds(off, block), cols]
                            key = kb * block + lax.broadcasted_iota(jnp.int32, (1, block), 1)
                            s = lax.dot_general(
                                qt, k, contract_last, preferred_element_type=jnp.float32
                            ) * factor
                            s = jnp.where((key >= start) & (key <= token), s, FLOOR)
                            new = jnp.maximum(top, jnp.max(s, axis=1, keepdims=True))
                            w = jnp.exp2(s - new)
                            shrink = jnp.exp2(top - new)
                            total = total * shrink + jnp.sum(w, axis=1, keepdims=True)
                            acc = acc * shrink + jnp.dot(
                                w.astype(jnp.bfloat16), v, preferred_element_type=jnp.float32
                            )
                            return (new, total, acc)

                        high = jnp.minimum(low + tile, end)
                        top, total, acc = lax.fori_loop(
                            start // block, (high + block - 1) // block, fold, (top, total, acc)
                        )
                        o = acc / total
                        for h in range(share):
                            place_to = slice((g * share + h) * D, (g * share + h + 1) * D)
                            part = slice(h * tile, (h + 1) * tile)
                            out[span, place_to] = jnp.where(
                                mine[part],
                                o[part],
                                out[span, place_to].astype(jnp.float32),
                            ).astype(out.dtype)


def local(
    ctx,
    queries,
    suffix_keys_values,
    cached_page_pool,
    prefix_page_hits,
    lengths,
    mamba_x,
    gate_z,
    delta,
    b_c,
    a_log,
    d_skip,
    state_pool,
    state_hits,
):
    tokens, width = mamba_x.shape
    states = a_log.shape[0]
    rows = width // LANES
    requests = lengths.shape[0]
    me = lax.axis_index("ctx")
    positions = me * tokens + jnp.arange(tokens, dtype=jnp.int32)
    segment, starts = segments_of(positions, lengths)
    opening = jnp.any(positions[:, None] == starts[None, :], axis=1).astype(jnp.int32)
    bounds = jnp.concatenate([starts, starts[-1:] + lengths[-1:]])[None, :]
    holder = starts // tokens
    opened = jnp.any(
        jnp.arange(ctx, dtype=jnp.int32)[:, None] == holder[None, :], axis=1
    ).astype(jnp.int32)[None, :]
    place = jnp.full((1, 1), me, jnp.int32)
    seg, opening = segment[None, :], opening[None, :]
    hits = state_hits[None, :]
    coeffs = b_c.reshape(2 * states, tokens)

    pages = lax.all_gather(cached_page_pool, "ctx")
    suffix = lax.all_gather(suffix_keys_values, "ctx")
    pool = lax.all_gather(state_pool.astype(jnp.bfloat16), "ctx", tiled=True)

    f32 = jnp.float32
    params = pltpu.CompilerParams(vmem_limit_bytes=56 * 1024 * 1024)
    scan_scratch = [
        pltpu.VMEM((tokens * rows, LANES), f32),
        pltpu.VMEM((tokens * rows, LANES), f32),
        pltpu.VMEM((states * rows, LANES), f32),
        pltpu.VMEM((requests, states * rows, LANES), f32),
    ]
    last, total = pl.pallas_call(
        last_state_kernel,
        out_shape=(
            jax.ShapeDtypeStruct((states * rows, LANES), f32),
            jax.ShapeDtypeStruct((rows, LANES), f32),
        ),
        in_specs=[VMEM] * 4 + [SMEM] * 4,
        out_specs=(VMEM, VMEM),
        scratch_shapes=scan_scratch,
        compiler_params=params,
        name="last_state",
    )(delta, mamba_x, a_log, pool, coeffs, seg, opening, hits)
    lasts = lax.all_gather(last.astype(jnp.bfloat16), "ctx")
    sums = lax.all_gather(total, "ctx")

    attended = pl.pallas_call(
        functools.partial(attention_kernel, math.gcd(tokens, 32), math.gcd(tokens, 128)),
        out_shape=jax.ShapeDtypeStruct(queries.shape, queries.dtype),
        in_specs=[VMEM] * 3 + [SMEM] * 3,
        out_specs=VMEM,
        scratch_shapes=[
            pltpu.VMEM(
                (
                    2,
                    prefix_page_hits.shape[1] * cached_page_pool.shape[2],
                    cached_page_pool.shape[3],
                ),
                jnp.bfloat16,
            )
        ],
        compiler_params=params,
        name="attention",
    )(queries, suffix, pages, prefix_page_hits, bounds, place)

    mixed = pl.pallas_call(
        mamba_kernel,
        out_shape=jax.ShapeDtypeStruct(mamba_x.shape, mamba_x.dtype),
        in_specs=[VMEM] * 8 + [SMEM] * 6,
        out_specs=VMEM,
        scratch_shapes=scan_scratch
        + [
            pltpu.VMEM((tokens * rows, LANES), f32),
            pltpu.VMEM((states * rows, LANES), f32),
        ],
        compiler_params=params,
        name="mamba",
    )(
        delta, mamba_x, a_log, gate_z, d_skip[None, :], pool, lasts, sums,
        coeffs, seg, opening, hits, opened, place,
    )
    return (attended, mixed)


def solution(mesh):
    placed = (
        P(("groups", "ctx"), "tp"),
        P(None, ("groups", "ctx"), "tp"),
        P(None, ("groups", "ctx"), None, "tp"),
        P("groups", None),
        P("groups"),
        P(("groups", "ctx"), "tp"),
        P(("groups", "ctx"), "tp"),
        P(("groups", "ctx"), "tp"),
        P(None, None, ("groups", "ctx")),
        P(None, "tp"),
        P("tp"),
        P(("groups", "ctx"), None, "tp"),
        P("groups"),
    )
    return jax.shard_map(
        functools.partial(local, mesh.shape["ctx"]),
        mesh=mesh,
        in_specs=placed,
        out_specs=(P(("groups", "ctx"), "tp"), P(("groups", "ctx"), "tp")),
        check_vma=False,
    )
```

time: 382 us -> 125 us (0.33); the launches traced: 378 us -> 125 us
  matrix products: 104 us -> 0 us
  local copies, waits for them, and re-layouts: 101 us -> 1.9 us
  other arithmetic: 87.8 us -> 5.84 us
  Pallas kernels: 0 us -> 36.6 us
  blocking collectives: 44.7 us -> 65 us
  loops' own time: 14.9 us -> 0 us
  waiting for transfers between devices: 10.5 us -> 0.68 us
    dot_general x75 -> x0, matrix products: 104 us -> none  [the longest x16 22.2 us: mamba_advance(): jnp.einsum('tr,rnd->tnd', select_blk, initial, precision=lax.Precision.HI...]
    reduce_sum x21 -> x0, other arithmetic: 51.8 us -> none  [the longest x16 35.8 us: mamba_advance(): within = jnp.sum(jnp.exp(gap) * drive[None], axis=1)]
    pallas_call x0 -> x3, Pallas kernels: none -> 36.6 us  [the longest x1 17.4 us: local(): pl.pallas_call(functools.partial(attention_kernel, math.gcd(tokens, 32),...]
    dynamic_update_slice x32 -> x0, local copies, waits for them, and re-layouts: 36.1 us -> none  [mamba_layer(): lax.scan(mamba_advance, start_carry, (blocked(step_size), blocked(inputs)...]
    all_gather x3 -> x4, blocking collectives: 44.7 us -> 65 us  [the longest x1 20.2 us: local(): pool = lax.all_gather(state_pool.astype(jnp.bfloat16), 'ctx', tiled=True)]
    mul x48 -> x0, local copies, waits for them, and re-layouts: 15 us -> none  [mamba_advance(): drive = step_blk[:, None, :] * in_blk[:, :, None] * input_blk[:, None, :]]
    another operation x3 -> x0, loops' own time: 14.9 us -> none  [the longest x1 12.1 us: mamba_layer(): lax.scan(mamba_advance, start_carry, (blocked(step_size), blocked(inputs)...]
    slice x50 -> x2, local copies, waits for them, and re-layouts: 16.4 us -> 1.89 us  [local(): bounds = jnp.concatenate([starts, starts[-1:] + lengths[-1:]])[None, :]]
  transfers between devices with their start and end apart: 2 -> 1, of which waited for: 1 -> 0; matrix products, arithmetic and copies ran while one was open for 60% -> 6% of each run, Pallas kernels for 0% -> 15%
where the time goes in v1:
time: 125 us
  blocking collectives  65 us (52%)
  Pallas kernels  36.6 us (29%)
  between operations  15.3 us (12%)
  other arithmetic  5.84 us (5%)
  local copies, waits for them, and re-layouts  1.9 us (2%)
    all_gather x1, blocking collectives, local(): pool = lax.all_gather(state_pool.astype(jnp.bfloat16), 'ctx', tiled=True)  20.2 us
    pallas_call x1, Pallas kernels, local(): pl.pallas_call(functools.partial(attention_kernel, math.gcd(tokens, 32),...  17.4 us
    all_gather x1, blocking collectives, local(): suffix = lax.all_gather(suffix_keys_values, 'ctx')  15.6 us
    all_gather x1, blocking collectives, local(): lasts = lax.all_gather(last.astype(jnp.bfloat16), 'ctx')  14.9 us
    all_gather x1, blocking collectives, local(): sums = lax.all_gather(total, 'ctx')  14.3 us
    pallas_call x1, Pallas kernels, local(): pl.pallas_call(mamba_kernel, out_shape=jax.ShapeDtypeStruct(mamba_x.shape...  11.2 us
    pallas_call x1, Pallas kernels, local(): pl.pallas_call(last_state_kernel, out_shape=(jax.ShapeDtypeStruct((states...  7.99 us
  transfers between devices with their start and end apart: 1, of which 0 were waited for; matrix products, arithmetic and copies ran while one was open for 6% of the time, Pallas kernels for 15%

profile of v1, /device:TPU:30, one launch (start us, length us, event | category | flops | bytes accessed | tf_op | source)
XLA Modules:
  0.0 125.4 jit_solution(5071076212519980801)
XLA Ops:
  7.2 0.0 all-gather.6.cloned.1.call-start
  7.2 0.7 all-gather.6.cloned.1.call-update
  7.9 1.3 %slice.7 = s32[1]{0:T(128)} slice(s32[4]{0:T(128)} %param.17), slice={[3:4]} | slice | bytes 8 | tf_op jit(solution)/shard_map/slice | solution.py:242
  9.2 0.8 reduce-window.9
  10.0 0.7 and_select_fusion
  10.7 0.6 slice.6
  11.3 1.0 convert_element_type.35
  12.3 0.1 convert_reduce_fusion
  12.4 0.1 compare_reduce_fusion
  12.4 20.2 %all_gather.31.pool = bf16[8,16,2048]{2,1,0:T(8,128)(2,1)} all-gather(bf16[2,16,2048]{2,1,0:T(8,128)(2,1)S(1)} %convert_element_type.35), channel_id=1, replica_groups=mesh['groups'=2,'ctx'=4,'tp'=4] {'ctx'}, dimensions={0}, use_global_device_ids=true | all-gather | bytes 655360 | tf_op jit(solution)/shard_map/all_gather | solution.py:254
  32.6 0.5 add_bitcast_fusion.1.seg
  33.2 0.5 convert_bitcast_fusion.1.opening
  33.7 8.0 %last_state.1 = (f32[256,128]{1,0:T(8,128)}, f32[16,128]{1,0:T(8,128)}) custom-call(bf16[128,2048]{1,0:T(8,128)(2,1)} %delta.3, bf16[128,2048]{1,0:T(8,128)(2,1)} %x.3, f32[16,2048]{1,0:T(8,128)} %a_log.3, bf16[8,16,2048]{2,1,0:T(8,128)(2,1)} %all_gather.31.pool, f32[32,128]{1,0:T(8,128)} %bitcast.24, s32[1,128]{1,0:T(1,128)} %add_bitcast_fusion.1.seg, ...), custom_call_target="tpu_custom_call" | custom-call | tf_op jit(solution)/shard_map/last_state/pallas_call | solution.py:264
  41.7 0.0 copy-start
  41.7 1.0 convert_element_type.39
  43.9 14.3 %all-gather.3 = f32[64,128]{1,0:T(8,128)} all-gather(f32[16,128]{1,0:T(8,128)} %get-tuple-element.5), channel_id=5, replica_groups=mesh['groups'=2,'ctx'=4,'tp'=4] {'ctx'}, dimensions={0}, use_global_device_ids=true | all-gather | bytes 40960 | tf_op jit(solution)/shard_map/all_gather | solution.py:277
  58.2 14.9 %all-gather.2 = bf16[1024,128]{1,0:T(8,128)(2,1)} all-gather(bf16[256,128]{1,0:T(8,128)(2,1)S(1)} %convert_element_type.39), channel_id=4, replica_groups=mesh['groups'=2,'ctx'=4,'tp'=4] {'ctx'}, dimensions={0}, use_global_device_ids=true | all-gather | bytes 327680 | tf_op jit(solution)/shard_map/all_gather | solution.py:276
  73.1 0.1 fusion
  73.3 0.5 convert_bitcast_fusion.opened
  73.8 11.2 %mamba.1 = bf16[128,2048]{1,0:T(8,128)(2,1)} custom-call(bf16[128,2048]{1,0:T(8,128)(2,1)} %delta.3, bf16[128,2048]{1,0:T(8,128)(2,1)} %x.3, f32[16,2048]{1,0:T(8,128)} %a_log.3, bf16[128,2048]{1,0:T(8,128)(2,1)} %gate.1, f32[1,2048]{1,0:T(1,128)} %bitcast.26, bf16[8,16,2048]{2,1,0:T(8,128)(2,1)} %all_gather.31.pool, bf16[4,256,128]{2,1,0:T(8,128)(2,1)} %bitcast.22, ...), custom_call_target="tpu_custom_call" | custom-call | tf_op jit(solution)/shard_map/mamba/pallas_call | solution.py:298
  85.0 0.6 add_bitcast_fusion.starts
  85.6 0.0 copy-done
  85.6 15.6 %all-gather = bf16[8,128,256]{2,1,0:T(8,128)(2,1)} all-gather(bf16[2,128,256]{2,1,0:T(8,128)(2,1)S(1)} %copy-done), channel_id=2, replica_groups=mesh['groups'=2,'ctx'=4,'tp'=4] {'ctx'}, dimensions={0}, use_global_device_ids=true | all-gather | bytes 655360 | tf_op jit(solution)/shard_map/all_gather | solution.py:253
  101.2 0.0 all-gather.6.cloned.1.call-done
  101.2 17.4 %attention.1 = bf16[128,2048]{1,0:T(8,128)(2,1)} custom-call(bf16[128,2048]{1,0:T(8,128)(2,1)} %q.1, bf16[4,2,128,256]{3,2,1,0:T(8,128)(2,1)} %bitcast.21, bf16[4,2,32,16,256]{4,3,2,1,0:T(8,128)(2,1)} %bitcast.20, s32[4,32]{1,0:T(4,128)} %hits.1, s32[1,5]{1,0:T(1,128)} %add_bitcast_fusion.starts, s32[1,1]{1,0:T(1,128)} %bitcast.5.place), custom_call_target="tpu_custom_call" | custom-call | tf_op jit(solution)/shard_map/attention/pallas_call | solution.py:279
  (1 shorter events, 0.0 us)
Async XLA Ops:
  7.2 94.0 %all-gather.6.cloned.1.call-start = ((), (), s32[]{:S(2)}) async-start(), calls=%async_computation | async-start | bytes 2621440 | tf_op jit(solution)/shard_map/all_gather | solution.py:252
  41.7 43.9 %copy-start = (bf16[2,128,256]{2,1,0:T(8,128)(2,1)S(1)}, bf16[2,128,256]{2,1,0:T(8,128)(2,1)}, u32[]{:S(2)}) copy-start(bf16[2,128,256]{2,1,0:T(8,128)(2,1)} %param.14) | copy-start | bytes 393220
Sparse Core Ops, SparseCore 0:
  9.6 51.7 all-gather.5

commit v2 on v1

--- a/solution.py
+++ b/solution.py
@@ -13,6 +13,7 @@
 LOG2E = math.log2(math.e)
 FLOOR = -1e30
 VMEM = pl.BlockSpec(memory_space=pltpu.VMEM)
+ANY = pl.BlockSpec(memory_space=pl.ANY)
 SMEM = pl.BlockSpec(memory_space=pltpu.SMEM)
 
 
@@ -46,12 +47,13 @@
         dt = dt_s[at, :]
         du = du_s[at, :]
         opens = opening[0, t] > 0
-        r = seg[0, t]
+        rates = rate_s[...]
+        begun = init_s[seg[0, t]]
         new, ys = [], []
         for n in range(states):
             part = slice(n * rows, (n + 1) * rows)
-            prior = jnp.where(opens, init_s[r, part, :], hs[n])
-            h = jnp.exp2(dt * rate_s[part, :]) * prior + du * b_c[n, t]
+            prior = jnp.where(opens, begun[part], hs[n])
+            h = jnp.exp2(dt * rates[part]) * prior + du * b_c[n, t]
             new.append(h)
             if y_s is not None:
                 ys.append(h * b_c[states + n, t])
@@ -84,45 +86,112 @@
             init_s[r, pl.ds(c, states, stride=rows), :] = chosen[:, c * LANES : (c + 1) * LANES]
 
 
-def last_state_kernel(
-    delta, x, a_log, pool, b_c, seg, opening, hits, last, dt_sum, dt_s, du_s, rate_s, init_s
+def exchange_kernel(
+    ctx,
+    delta, x, a_log, gate, d_skip, pool, b_c, seg, opening, hits, opened, pages, suffix,
+    out, pages_all, suffix_all,
+    dt_s, du_s, rate_s, init_s, y_s, enter_s, pool_s, mine_s, lasts_s, total_s, totals_s,
+    own_sem, page_sem, suffix_sem, pool_sem, last_sem, total_sem,
 ):
     tokens, width = delta.shape
     rows, states = width // LANES, a_log.shape[0]
+    slots = pool.shape[0]
+    me = lax.axis_index("ctx")
+    peers = range(1, ctx)
+
+    own = [
+        pltpu.make_async_copy(pages, pages_all.at[me], own_sem.at[0]),
+        pltpu.make_async_copy(suffix, suffix_all.at[me], own_sem.at[1]),
+    ]
+    for copy in own:
+        copy.start()
+    held = pl.ds(me * slots, slots)
+    pool_s[held] = pool[...].astype(jnp.bfloat16)
+
+    def remote(source, target, sems, d):
+        return pltpu.make_async_remote_copy(
+            src_ref=source,
+            dst_ref=target,
+            send_sem=sems.at[0, d - 1],
+            recv_sem=sems.at[1, d - 1],
+            device_id={"ctx": lax.rem(me + d, ctx)},
+            device_id_type=pl.DeviceIdType.MESH,
+        )
+
+    barrier = pltpu.get_barrier_semaphore()
+    for d in peers:
+        pl.semaphore_signal(
+            barrier,
+            inc=1,
+            device_id={"ctx": lax.rem(me + d, ctx)},
+            device_id_type=pl.DeviceIdType.MESH,
+        )
+    pl.semaphore_wait(barrier, ctx - 1)
+
+    pool_copies = [remote(pool_s.at[held], pool_s.at[held], pool_sem, d) for d in peers]
+    page_copies = [remote(pages, pages_all.at[me], page_sem, d) for d in peers]
+    suffix_copies = [remote(suffix, suffix_all.at[me], suffix_sem, d) for d in peers]
+    last_copies = [remote(mine_s, lasts_s.at[d - 1], last_sem, d) for d in peers]
+    total_copies = [remote(total_s, totals_s.at[d - 1], total_sem, d) for d in peers]
+    for copy in pool_copies:
+        copy.start()
+    for copy in page_copies:
+        copy.start()
+    for d in peers:
+
+        @pl.when(me + d < ctx)
+        def _():
+            suffix_copies[d - 1].start()
+
     spread_inputs(delta, x, a_log, dt_s, du_s, rate_s)
-    load_initials(pool, hits, init_s, rows)
+    for copy in pool_copies:
+        copy.wait_recv()
+    load_initials(pool_s, hits, init_s, rows)
     zeros = [jnp.zeros((rows, LANES), jnp.float32)] * states
     hs, total = scan_tokens(
         tokens, rows, states, dt_s, du_s, rate_s, init_s, b_c, seg, opening, zeros, None
     )
-    for n in range(states):
-        last[n * rows : (n + 1) * rows, :] = hs[n]
-    dt_sum[...] = total
-
-
-def mamba_kernel(
-    delta, x, a_log, gate, d_skip, pool, lasts, sums, b_c, seg, opening, hits, opened, place,
-    out, dt_s, du_s, rate_s, init_s, y_s, enter_s,
-):
-    tokens, width = delta.shape
-    rows, states = width // LANES, a_log.shape[0]
-    spread_inputs(delta, x, a_log, dt_s, du_s, rate_s)
-    load_initials(pool, hits, init_s, rows)
+    mine_s[...] = jnp.concatenate(hs, axis=0).astype(jnp.bfloat16)
+    total_s[...] = total
+    for d in peers:
+
+        @pl.when(me + d < ctx)
+        def _():
+            last_copies[d - 1].start()
+            total_copies[d - 1].start()
+
     enter_s[...] = jnp.zeros_like(enter_s)
-
-    def join(j, carry):
-        kept = jnp.where(opened[0, j] > 0, 0.0, 1.0)
-        total = sums[j]
-        for n in range(states):
-            part = slice(n * rows, (n + 1) * rows)
-            decay = jnp.exp2(total * rate_s[part, :]) * kept
-            enter_s[part, :] = decay * enter_s[part, :] + lasts[j, part, :].astype(jnp.float32)
-        return carry
-
-    lax.fori_loop(0, place[0, 0], join, 0)
+    for d in reversed(peers):
+
+        @pl.when(me >= d)
+        def _():
+            last_copies[d - 1].wait_recv()
+            total_copies[d - 1].wait_recv()
+            kept = jnp.where(opened[0, me - d] > 0, 0.0, 1.0)
+            sums = jnp.concatenate([totals_s[d - 1]] * states, axis=0)
+            decay = jnp.exp2(sums * rate_s[...]) * kept
+            enter_s[...] = decay * enter_s[...] + lasts_s[d - 1].astype(jnp.float32)
+
     hs = [enter_s[n * rows : (n + 1) * rows, :] for n in range(states)]
     scan_tokens(tokens, rows, states, dt_s, du_s, rate_s, init_s, b_c, seg, opening, hs, y_s)
     gate_outputs(x, gate, d_skip, y_s, out)
+
+    for d in peers:
+
+        @pl.when(me >= d)
+        def _():
+            suffix_copies[d - 1].wait_recv()
+
+        @pl.when(me + d < ctx)
+        def _():
+            suffix_copies[d - 1].wait_send()
+            last_copies[d - 1].wait_send()
+            total_copies[d - 1].wait_send()
+
+        pool_copies[d - 1].wait_send()
+        page_copies[d - 1].wait()
+    for copy in own:
+        copy.wait()
 
 
 def attention_kernel(tile, block, q, suffix, pages, hits, starts, place, out, kept):
@@ -249,32 +318,48 @@
     hits = state_hits[None, :]
     coeffs = b_c.reshape(2 * states, tokens)
 
-    pages = lax.all_gather(cached_page_pool, "ctx")
-    suffix = lax.all_gather(suffix_keys_values, "ctx")
-    pool = lax.all_gather(state_pool.astype(jnp.bfloat16), "ctx", tiled=True)
-
-    f32 = jnp.float32
+    f32, bf16 = jnp.float32, jnp.bfloat16
     params = pltpu.CompilerParams(vmem_limit_bytes=56 * 1024 * 1024)
-    scan_scratch = [
-        pltpu.VMEM((tokens * rows, LANES), f32),
-        pltpu.VMEM((tokens * rows, LANES), f32),
-        pltpu.VMEM((states * rows, LANES), f32),
-        pltpu.VMEM((requests, states * rows, LANES), f32),
-    ]
-    last, total = pl.pallas_call(
-        last_state_kernel,
+    slots = state_pool.shape[0]
+    sems = pltpu.SemaphoreType.DMA((2, ctx - 1))
+    whole = pltpu.VMEM((tokens * rows, LANES), f32)
+    state = pltpu.VMEM((states * rows, LANES), f32)
+    mixed, pages, suffix = pl.pallas_call(
+        functools.partial(exchange_kernel, ctx),
         out_shape=(
-            jax.ShapeDtypeStruct((states * rows, LANES), f32),
-            jax.ShapeDtypeStruct((rows, LANES), f32),
+            jax.ShapeDtypeStruct(mamba_x.shape, mamba_x.dtype),
+            jax.ShapeDtypeStruct((ctx,) + cached_page_pool.shape, bf16),
+            jax.ShapeDtypeStruct((ctx,) + suffix_keys_values.shape, bf16),
         ),
-        in_specs=[VMEM] * 4 + [SMEM] * 4,
-        out_specs=(VMEM, VMEM),
-        scratch_shapes=scan_scratch,
-        compiler_params=params,
-        name="last_state",
-    )(delta, mamba_x, a_log, pool, coeffs, seg, opening, hits)
-    lasts = lax.all_gather(last.astype(jnp.bfloat16), "ctx")
-    sums = lax.all_gather(total, "ctx")
+        in_specs=[VMEM] * 6 + [SMEM] * 5 + [ANY] * 2,
+        out_specs=(VMEM, ANY, ANY),
+        scratch_shapes=[
+            whole,
+            whole,
+            state,
+            pltpu.VMEM((requests, states * rows, LANES), f32),
+            whole,
+            state,
+            pltpu.VMEM((ctx * slots, states, width), bf16),
+            pltpu.VMEM((states * rows, LANES), bf16),
+            pltpu.VMEM((ctx - 1, states * rows, LANES), bf16),
+            pltpu.VMEM((rows, LANES), f32),
+            pltpu.VMEM((ctx - 1, rows, LANES), f32),
+            pltpu.SemaphoreType.DMA((2,)),
+            sems,
+            sems,
+            sems,
+            sems,
+            sems,
+        ],
+        compiler_params=pltpu.CompilerParams(
+            collective_id=0, has_side_effects=True, vmem_limit_bytes=56 * 1024 * 1024
+        ),
+        name="exchange_and_mamba",
+    )(
+        delta, mamba_x, a_log, gate_z, d_skip[None, :], state_pool,
+        coeffs, seg, opening, hits, opened, cached_page_pool, suffix_keys_values,
+    )
 
     attended = pl.pallas_call(
         functools.partial(attention_kernel, math.gcd(tokens, 32), math.gcd(tokens, 128)),
@@ -295,22 +380,6 @@
         name="attention",
     )(queries, suffix, pages, prefix_page_hits, bounds, place)
 
-    mixed = pl.pallas_call(
-        mamba_kernel,
-        out_shape=jax.ShapeDtypeStruct(mamba_x.shape, mamba_x.dtype),
-        in_specs=[VMEM] * 8 + [SMEM] * 6,
-        out_specs=VMEM,
-        scratch_shapes=scan_scratch
-        + [
-            pltpu.VMEM((tokens * rows, LANES), f32),
-            pltpu.VMEM((states * rows, LANES), f32),
-        ],
-        compiler_params=params,
-        name="mamba",
-    )(
-        delta, mamba_x, a_log, gate_z, d_skip[None, :], pool, lasts, sums,
-        coeffs, seg, opening, hits, opened, place,
-    )
     return (attended, mixed)
 
 

time: 125 us -> 112 us (0.90); the launches traced: 125 us -> 110 us
  blocking collectives: 65 us -> 0 us
  Pallas kernels: 36.6 us -> 101 us
  between operations: 15.3 us -> 2 us
  other arithmetic: 5.84 us -> 3.97 us
    pallas_call x2 -> x1, Pallas kernels: 19.2 us -> 86.9 us  [local(): pl.pallas_call(functools.partial(exchange_kernel, ctx), out_shape=(jax.Sh...]
    all_gather x4 -> x0, blocking collectives: 65 us -> none  [the longest x1 20.2 us: local(): pool = lax.all_gather(state_pool.astype(jnp.bfloat16), 'ctx', tiled=True)]
    pallas_call x1, Pallas kernels: 17.4 us -> 14.2 us  [local(): pl.pallas_call(functools.partial(attention_kernel, math.gcd(tokens, 32),...]
    convert_element_type x2 -> x0, other arithmetic: 1.92 us -> none  [the longest x1 0.96 us: local(): pool = lax.all_gather(state_pool.astype(jnp.bfloat16), 'ctx', tiled=True)]
  transfers between devices with their start and end apart: 1 -> 0, of which waited for: 0 -> 0; matrix products, arithmetic and copies ran while one was open for 6% -> 0% of each run, Pallas kernels for 15% -> 0%
where the time goes in v2:
time: 112 us; the launch traced here: 110 us
  Pallas kernels  101 us (90%)
  other arithmetic  3.97 us (4%)
  local copies, waits for them, and re-layouts  2.7 us (2%)
  between operations  2 us (2%)
    pallas_call x1, Pallas kernels, local(): pl.pallas_call(functools.partial(exchange_kernel, ctx), out_shape=(jax.Sh...  86.9 us
    pallas_call x1, Pallas kernels, local(): pl.pallas_call(functools.partial(attention_kernel, math.gcd(tokens, 32),...  14.2 us

profile of v2, /device:TPU:30, one launch (start us, length us, event | category | flops | bytes accessed | tf_op | source)
XLA Modules:
  0.0 109.8 jit_solution(304311184103630749)
XLA Ops:
  0.6 1.3 %slice.7 = s32[1]{0:T(128)} slice(s32[4]{0:T(128)} %param.17), slice={[3:4]} | slice | bytes 8 | tf_op jit(solution)/shard_map/slice | solution.py:311
  2.0 0.8 reduce-window.9
  2.8 0.7 and_select_fusion
  3.4 0.6 slice.6
  5.4 0.1 fusion
  5.5 0.5 convert_bitcast_fusion.opened
  6.0 0.6 add_bitcast_fusion.starts
  6.6 0.1 compare_reduce_fusion
  6.7 0.1 convert_reduce_fusion
  6.7 0.5 add_bitcast_fusion.1.seg
  7.3 0.6 convert_bitcast_fusion.1.opening
  7.8 86.9 %exchange_and_mamba.1 = (bf16[128,2048]{1,0:T(8,128)(2,1)}, bf16[4,2,32,16,256]{4,3,2,1,0:T(8,128)(2,1)}, bf16[4,2,128,256]{3,2,1,0:T(8,128)(2,1)}) custom-call(bf16[128,2048]{1,0:T(8,128)(2,1)} %delta.1, bf16[128,2048]{1,0:T(8,128)(2,1)} %x.1, f32[16,2048]{1,0:T(8,128)} %a_log.1, bf16[128,2048]{1,0:T(8,128)(2,1)} %gate.1, f32[1,2048]{1,0:T(1,128)} %bitcast.17, ...), custom_call_target="tpu_custom_call" | custom-call | tf_op jit(solution)/shard_map/exchange_and_mamba/pallas_call | solution.py:327
  94.7 0.0 copy-start
  94.8 14.2 %attention.1 = bf16[128,2048]{1,0:T(8,128)(2,1)} custom-call(bf16[128,2048]{1,0:T(8,128)(2,1)} %q.1, bf16[4,2,128,256]{3,2,1,0:T(8,128)(2,1)} %get-tuple-element.5.suffix, bf16[4,2,32,16,256]{4,3,2,1,0:T(8,128)(2,1)} %get-tuple-element.6.pages, s32[4,32]{1,0:T(4,128)} %hits.1, s32[1,5]{1,0:T(1,128)} %add_bitcast_fusion.starts, s32[1,1]{1,0:T(1,128)} %bitcast.9.place), custom_call_target="tpu_custom_call" | custom-call | tf_op jit(solution)/shard_map/attention/pallas_call | solution.py:364
  109.0 0.0 copy-done
  109.0 0.8 copy.16
  (1 shorter events, 0.0 us)
Async XLA Ops:
  94.7 14.2 %copy-start = (bf16[128,2048]{1,0:T(8,128)(2,1)S(1)}, bf16[128,2048]{1,0:T(8,128)(2,1)}, u32[]{:S(2)}) copy-start(bf16[128,2048]{1,0:T(8,128)(2,1)} %get-tuple-element.13) | copy-start | bytes 1572868

commit v3 on v2

--- a/solution.py
+++ b/solution.py
@@ -18,8 +18,9 @@
 
 
 def segments_of(positions, lengths):
-    ends = jnp.cumsum(lengths)
-    starts = ends - lengths
+    order = jnp.arange(lengths.shape[0], dtype=jnp.int32)
+    earlier = order[None, :] < order[:, None]
+    starts = jnp.sum(jnp.where(earlier, lengths[None, :], 0), axis=1)
     member = (positions[:, None] >= starts[None, :]).astype(jnp.int32)
     return (jnp.sum(member, axis=1) - 1, starts)
 
@@ -129,14 +130,51 @@
     pl.semaphore_wait(barrier, ctx - 1)
 
     pool_copies = [remote(pool_s.at[held], pool_s.at[held], pool_sem, d) for d in peers]
-    page_copies = [remote(pages, pages_all.at[me], page_sem, d) for d in peers]
+
+    def hop(way, step, half, shard):
+        source = pages.at[half] if step == 1 else pages_all.at[shard, half]
+        return pltpu.make_async_remote_copy(
+            src_ref=source,
+            dst_ref=pages_all.at[shard, half],
+            send_sem=page_sem.at[0, way, half, step - 1],
+            recv_sem=page_sem.at[1, way, half, step - 1],
+            device_id={"ctx": lax.rem(me + (1 if way == 0 else ctx - 1), ctx)},
+            device_id_type=pl.DeviceIdType.MESH,
+        )
+
+    def sends(way, step):
+        if way == 0:
+            return me - (step - 1), (me + 1 < ctx) & (me - (step - 1) >= 0)
+        return me + (step - 1), (me >= 1) & (me + (step - 1) < ctx)
+
+    def begin(step, half):
+        for way in range(2):
+            shard, valid = sends(way, step)
+
+            @pl.when(valid)
+            def _():
+                hop(way, step, half, shard).start()
+
+    def advance(step):
+        for half in range(2):
+            for way in range(2):
+                shard = me - step if way == 0 else me + step
+
+                @pl.when((shard >= 0) & (shard < ctx))
+                def _():
+                    hop(way, step, half, shard).wait_recv()
+
+            if step + 1 < ctx:
+                begin(step + 1, half)
+
     suffix_copies = [remote(suffix, suffix_all.at[me], suffix_sem, d) for d in peers]
     last_copies = [remote(mine_s, lasts_s.at[d - 1], last_sem, d) for d in peers]
     total_copies = [remote(total_s, totals_s.at[d - 1], total_sem, d) for d in peers]
     for copy in pool_copies:
         copy.start()
-    for copy in page_copies:
-        copy.start()
+    if ctx > 1:
+        for half in range(2):
+            begin(1, half)
     for d in peers:
 
         @pl.when(me + d < ctx)
@@ -160,6 +198,8 @@
             last_copies[d - 1].start()
             total_copies[d - 1].start()
 
+    if ctx > 1:
+        advance(1)
     enter_s[...] = jnp.zeros_like(enter_s)
     for d in reversed(peers):
 
@@ -174,7 +214,20 @@
 
     hs = [enter_s[n * rows : (n + 1) * rows, :] for n in range(states)]
     scan_tokens(tokens, rows, states, dt_s, du_s, rate_s, init_s, b_c, seg, opening, hs, y_s)
+    if ctx > 2:
+        advance(2)
     gate_outputs(x, gate, d_skip, y_s, out)
+    for step in range(3, ctx):
+        advance(step)
+
+    for step in peers:
+        for way in range(2):
+            shard, valid = sends(way, step)
+
+            @pl.when(valid)
+            def _():
+                for half in range(2):
+                    hop(way, step, half, shard).wait_send()
 
     for d in peers:
 
@@ -189,7 +242,6 @@
             total_copies[d - 1].wait_send()
 
         pool_copies[d - 1].wait_send()
-        page_copies[d - 1].wait()
     for copy in own:
         copy.wait()
 
@@ -346,7 +398,7 @@
             pltpu.VMEM((rows, LANES), f32),
             pltpu.VMEM((ctx - 1, rows, LANES), f32),
             pltpu.SemaphoreType.DMA((2,)),
-            sems,
+            pltpu.SemaphoreType.DMA((2, 2, 2, ctx - 1)),
             sems,
             sems,
             sems,

time: 112 us -> 87.3 us (0.78)
  Pallas kernels: 101 us -> 77.6 us
    pallas_call x1, Pallas kernels: 86.9 us -> 63.9 us  [local(): pl.pallas_call(functools.partial(exchange_kernel, ctx), out_shape=(jax.Sh...]
where the time goes in v3:
time: 87.3 us; the launch traced here: 85.6 us
  Pallas kernels  77.6 us (89%)
  other arithmetic  3.26 us (4%)
  local copies, waits for them, and re-layouts  2.7 us (3%)
  between operations  2 us (2%)
    pallas_call x1, Pallas kernels, local(): pl.pallas_call(functools.partial(exchange_kernel, ctx), out_shape=(jax.Sh...  63.9 us
    pallas_call x1, Pallas kernels, local(): pl.pallas_call(functools.partial(attention_kernel, math.gcd(tokens, 32),...  13.8 us
    slice x2, local copies, waits for them, and re-layouts, local(): bounds = jnp.concatenate([starts, starts[-1:] + lengths[-1:]])[None, :]  1.9 us

profile of v3, /device:TPU:30, one launch (start us, length us, event | category | flops | bytes accessed | tf_op | source)
XLA Modules:
  0.0 85.6 jit_solution(6674109864140793535)
XLA Ops:
  0.6 1.3 %slice.7 = s32[1]{0:T(128)} slice(s32[4]{0:T(128)} %param.17), slice={[3:4]} | slice | bytes 8 | tf_op jit(solution)/shard_map/slice | solution.py:363
  2.0 0.8 select_reduce_fusion
  2.7 0.6 slice.6
  4.7 0.6 add_bitcast_fusion.starts
  5.2 0.1 compare_reduce_fusion
  5.3 0.1 convert_reduce_fusion
  5.4 0.1 fusion
  5.5 0.6 convert_bitcast_fusion.opened
  6.1 0.5 add_bitcast_fusion.1.seg
  6.6 0.5 convert_bitcast_fusion.1.opening
  7.2 63.9 %exchange_and_mamba.1 = (bf16[128,2048]{1,0:T(8,128)(2,1)}, bf16[4,2,32,16,256]{4,3,2,1,0:T(8,128)(2,1)}, bf16[4,2,128,256]{3,2,1,0:T(8,128)(2,1)}) custom-call(bf16[128,2048]{1,0:T(8,128)(2,1)} %delta.1, bf16[128,2048]{1,0:T(8,128)(2,1)} %x.1, f32[16,2048]{1,0:T(8,128)} %a_log.1, bf16[128,2048]{1,0:T(8,128)(2,1)} %gate.1, f32[1,2048]{1,0:T(1,128)} %bitcast.13, ...), custom_call_target="tpu_custom_call" | custom-call | tf_op jit(solution)/shard_map/exchange_and_mamba/pallas_call | solution.py:379
  71.0 0.0 copy-start
  71.0 13.8 %attention.1 = bf16[128,2048]{1,0:T(8,128)(2,1)} custom-call(bf16[128,2048]{1,0:T(8,128)(2,1)} %q.1, bf16[4,2,128,256]{3,2,1,0:T(8,128)(2,1)} %get-tuple-element.5.suffix, bf16[4,2,32,16,256]{4,3,2,1,0:T(8,128)(2,1)} %get-tuple-element.6.pages, s32[4,32]{1,0:T(4,128)} %hits.1, s32[1,5]{1,0:T(1,128)} %add_bitcast_fusion.starts, s32[1,1]{1,0:T(1,128)} %bitcast.7.place), custom_call_target="tpu_custom_call" | custom-call | tf_op jit(solution)/shard_map/attention/pallas_call | solution.py:416
  84.8 0.0 copy-done
  84.8 0.8 copy.16
  (2 shorter events, 0.0 us)
Async XLA Ops:
  71.0 13.8 %copy-start = (bf16[128,2048]{1,0:T(8,128)(2,1)S(1)}, bf16[128,2048]{1,0:T(8,128)(2,1)}, u32[]{:S(2)}) copy-start(bf16[128,2048]{1,0:T(8,128)(2,1)} %get-tuple-element.11) | copy-start | bytes 1572868
